TPU v7x, 32 devices: a whole 2x2x4 slice. The times are simulated.
32 devices in a mesh: seq: 16 (over z, y, x), tp: 2 (over core).
Axes of the slice: x: 2, y: 2, z: 4, core: 2. Of those that a mesh axis runs over, the one named last changes fastest.
Arguments:
- queries: bfloat16 [4096, 4096], P('seq', 'tp'), may hold values from -6 to 6
- keys: bfloat16 [4096, 4096], P('seq', 'tp'), may hold values from -6 to 6
- values: bfloat16 [4096, 4096], P('seq', 'tp'), may hold values from -6 to 6
- out_cotangent: bfloat16 [4096, 2048], P('seq', 'tp'), may hold values from -6 to 6
- proj_weight: bfloat16 [4096, 2048], P('tp', 'seq'), may hold values from -0.125 to 0.125
Outputs:
- grad_queries: bfloat16 [4096, 4096], P('seq', 'tp')
- grad_keys: bfloat16 [4096, 4096], P('seq', 'tp')
- grad_values: bfloat16 [4096, 4096], P('seq', 'tp')
- grad_proj: float32 [4096, 2048], P('tp', 'seq')
All inputs are finite; a program needn't handle non-finite values.
Results may differ from a plain program's by a relative error of at most 0.0058.
Values may be sent and summed in bfloat16 or wider, within the bound.
A program may use at most 128 MiB of HBM per device.

v0:
```python
import jax
import jax.numpy as jnp
from jax import lax
from jax.sharding import PartitionSpec as P

DH = 128


def entering(part, axis, combine, identity, reverse):
    count = lax.axis_size(axis)
    place = lax.axis_index(axis)
    ahead = count - 1 - place if reverse else place
    gathered = lax.all_gather(part, axis)
    state = jnp.zeros_like(part) + jnp.asarray(identity, part.dtype)

    def one(step, state):
        source = count - 1 - step if reverse else step
        return combine(state, lax.dynamic_index_in_dim(gathered, source, 0, False))

    return lax.fori_loop(0, ahead, one, state)


def add_pair(earlier, later_one):
    return earlier + later_one


def per_device(queries, keys, values, out_cotangent, proj_weight):
    tok = queries.shape[0]
    heads = queries.shape[1] // DH
    seq_count = lax.axis_size("seq")
    scale = 1.0 / jnp.sqrt(jnp.float32(DH * tok * seq_count))
    q_heads = queries.reshape(tok, heads, DH)
    k_heads = keys.reshape(tok, heads, DH)
    v_heads = values.reshape(tok, heads, DH)
    kv_state = jnp.einsum("thd,the->hde", k_heads, v_heads, preferred_element_type=jnp.float32)
    zero_state = jnp.zeros_like(kv_state)
    prior_sum = entering(kv_state, "seq", add_pair, zero_state, False)
    full_cot = lax.all_gather(out_cotangent, "tp", axis=1, tiled=True)
    grad_out = lax.dot_general(
        full_cot,
        lax.all_gather(proj_weight, "seq", axis=1, tiled=True),
        (((1,), (1,)), ((), ())),
        preferred_element_type=jnp.float32,
    ).astype(jnp.bfloat16)
    g_heads = grad_out.reshape(tok, heads, DH)
    qg_state = jnp.einsum("thd,the->hde", q_heads, g_heads, preferred_element_type=jnp.float32)
    later_sum = entering(qg_state, "seq", add_pair, zero_state, True)
    prior = prior_sum.astype(jnp.bfloat16)
    later = later_sum.astype(jnp.bfloat16)
    rows = jnp.arange(tok)
    causal = (rows[:, None] >= rows[None, :])[None]
    attn = jnp.where(
        causal,
        jnp.einsum("thd,shd->hts", q_heads, k_heads, preferred_element_type=jnp.float32),
        0.0,
    ).astype(jnp.bfloat16)
    back = jnp.where(
        causal,
        jnp.einsum("thd,shd->hts", g_heads, v_heads, preferred_element_type=jnp.float32),
        0.0,
    ).astype(jnp.bfloat16)
    attn_out = scale * (
        jnp.einsum("hts,she->the", attn, v_heads, preferred_element_type=jnp.float32)
        + jnp.einsum("thd,hde->the", q_heads, prior, preferred_element_type=jnp.float32)
    )
    grad_q = scale * (
        jnp.einsum("hts,shd->thd", back, k_heads, preferred_element_type=jnp.float32)
        + jnp.einsum("the,hde->thd", g_heads, prior, preferred_element_type=jnp.float32)
    )
    grad_k = scale * (
        jnp.einsum("hts,thd->shd", back, q_heads, preferred_element_type=jnp.float32)
        + jnp.einsum("she,hde->shd", v_heads, later, preferred_element_type=jnp.float32)
    )
    grad_v = scale * (
        jnp.einsum("hts,the->she", attn, g_heads, preferred_element_type=jnp.float32)
        + jnp.einsum("shd,hde->she", k_heads, later, preferred_element_type=jnp.float32)
    )
    out_flat = attn_out.astype(jnp.bfloat16).reshape(tok, heads * DH)
    proj_term = lax.dot_general(
        out_flat, full_cot, (((0,), (0,)), ((), ())), preferred_element_type=jnp.float32
    )
    proj_sum = lax.psum_scatter(proj_term, "seq", scatter_dimension=1, tiled=True)
    grad_proj = proj_sum / jnp.sqrt(jnp.float32(tok * seq_count))
    width = heads * DH
    return (
        grad_q.astype(jnp.bfloat16).reshape(tok, width),
        grad_k.astype(jnp.bfloat16).reshape(tok, width),
        grad_v.astype(jnp.bfloat16).reshape(tok, width),
        grad_proj,
    )


def solution(mesh):
    return jax.shard_map(
        per_device,
        mesh=mesh,
        in_specs=(P("seq", "tp"), P("seq", "tp"), P("seq", "tp"), P("seq", "tp"), P("tp", "seq")),
        out_specs=(P("seq", "tp"), P("seq", "tp"), P("seq", "tp"), P("tp", "seq")),
        check_vma=False,
    )
```

profile of v0, /device:TPU:0, one launch (start us, length us, event | category | flops | bytes accessed | tf_op | source)
XLA Modules:
  0.0 908.8 jit_solution(14762071667851500176)
XLA Ops:
  7.2 0.0 copy-start
  7.2 0.0 copy-start.3
  7.2 0.0 all-gather.7.cloned.1.call-start
  7.2 0.7 all-gather.7.cloned.1.call-update
  7.9 0.0 all-gather.9.cloned.1.call-start
  8.0 0.7 all-gather.9.cloned.1.call-update
  8.7 0.0 all-gather.11.cloned.1.call-start
  8.7 1.5 copy.56
  10.2 1.5 fusion.11
  11.7 0.0 all-gather.11.cloned.1.call-update
  11.7 0.0 all-gather.13.cloned.1.call-start
  11.7 9.6 %all-gather.7.cloned.1.call-done = bf16[256,2048]{1,0:T(8,128)(2,1)} async-done(((bf16[256,1024]{1,0:T(8,128)(2,1)}), bf16[256,2048]{1,0:T(8,128)(2,1)}) %all-gather.7.cloned.1.call-update) | async-done | bytes 1048592 | tf_op jit(solution)/shard_map/all_gather | solution.py:38
  21.3 146.3 %all-gather.9.cloned.1.call-done = bf16[2048,2048]{1,0:T(8,128)(2,1)} async-done(((bf16[2048,128]{1,0:T(8,128)(2,1)}), bf16[2048,2048]{1,0:T(8,128)(2,1)}) %all-gather.9.cloned.1.call-update) | async-done | bytes 8388624 | tf_op jit(solution)/shard_map/all_gather | solution.py:41
  167.6 7.1 convolution_convert_fusion
  174.6 1.5 copy.55
  176.1 0.0 copy-start.1
  176.1 0.0 copy-done
  176.2 1.4 convolution_bitcast_fusion
  177.5 2.7 copy.40
  180.2 0.0 copy-done.1
  180.2 0.0 all-gather.13.cloned.1.call-update
  180.3 0.0 reduce-scatter.2.cloned.1.call-start
  180.4 1.9 select_convert_fusion
  182.3 0.0 copy-start.6
  182.3 1.3 copy-done.6
  183.6 2.2 fusion.30
  185.8 175.0 %all-gather.11.cloned.1.call-done = f32[256,128,128]{2,1,0:T(8,128)} async-done(((f32[16,128,128]{2,1,0:T(8,128)}), f32[256,128,128]{2,1,0:T(8,128)}) %all-gather.11.cloned.1.call-update) | async-done | bytes 16777232 | tf_op jit(solution)/shard_map/all_gather | solution.py:13
  360.8 0.1 broadcast_in_dim.26.clone
  360.9 2.2 fusion.1
  363.1 9.0 fusion.31
  372.1 0.0 reduce-scatter.2.cloned.1.call-update
  372.1 0.0 copy-start.4
  372.1 2.1 select_convert_fusion.1
  374.2 0.8 fusion.13
  375.0 0.0 copy-start.2
  375.1 1.9 fusion.6
  377.0 0.7 copy-done.7
  377.7 1.7 fusion.29
  379.5 1.4 fusion.5
  380.9 2.3 copy.50
  383.2 170.1 %all-gather.13.cloned.1.call-done = f32[256,128,128]{2,1,0:T(8,128)} async-done(((f32[16,128,128]{2,1,0:T(8,128)}), f32[256,128,128]{2,1,0:T(8,128)}) %all-gather.13.cloned.1.call-update) | async-done | bytes 16777232 | tf_op jit(solution)/shard_map/all_gather | solution.py:13
  553.2 0.1 broadcast_in_dim.26.clone.1
  553.3 23.0 %while.23 = (s32[]{:T(128)}, f32[16,128,128]{2,1,0:T(8,128)S(1)}, s32[]{:T(128)}, f32[16,16,128,128]{3,2,1,0:T(8,128)}, s32[]{:T(128)}, /*index=5*/s32[]{:T(128)}, s32[]{:T(128)}, s32[]{:T(128)}) while((s32[]{:T(128)}, f32[16,128,128]{2,1,0:T(8,128)S(1)}, s32[]{:T(128)}, f32[16,16,128,128]{3,2,1,0:T(8,128)}, s32[]{:T(128)}, ...), condition=%wide.region_3.4_spmd, body=%wide.region_2.3_spmd.sunk | while | flops 262150 | bytes 3145871 | solution.py:20
  553.4 1.5 bitcast_add_fusion.8
  554.9 1.5 bitcast_add_fusion.8
  556.4 1.5 bitcast_add_fusion.8
  557.9 1.5 bitcast_add_fusion.8
  559.4 1.8 bitcast_add_fusion.8
  561.2 1.5 bitcast_add_fusion.8
  562.7 1.5 bitcast_add_fusion.8
  564.2 1.5 bitcast_add_fusion.8
  565.7 1.5 bitcast_add_fusion.8
  567.2 1.5 bitcast_add_fusion.8
  568.7 1.5 bitcast_add_fusion.8
  570.3 1.5 bitcast_add_fusion.8
  571.8 1.5 bitcast_add_fusion.8
  573.3 1.5 bitcast_add_fusion.8
  574.8 1.5 bitcast_add_fusion.8
  576.3 3.0 fusion.3
  579.3 2.4 copy.51
  581.7 3.1 multiply_convert_fusion
  584.7 2.3 copy.52
  587.0 313.0 %reduce-scatter.2.cloned.1.call-done = f32[2048,128]{1,0:T(8,128)} async-done(((f32[2048,2048]{1,0:T(8,128)}), f32[2048,128]{1,0:T(8,128)}) %reduce-scatter.2.cloned.1.call-update) | async-done | bytes 1048592 | tf_op jit(solution)/shard_map/reduce_scatter | solution.py:82
  900.0 2.3 broadcast_multiply_fusion
  (10 shorter events, 0.1 us)
Async XLA Ops:
  7.2 169.0 %copy-start = (bf16[256,2048]{1,0:T(8,128)(2,1)S(1)}, bf16[256,2048]{1,0:T(8,128)(2,1)}, u32[]{:S(2)}) copy-start(bf16[256,2048]{1,0:T(8,128)(2,1)} %param.9) | copy-start | bytes 3145732
  7.2 3.0 copy-start.3
  7.2 14.1 %all-gather.7.cloned.1.call-start = ((), (), s32[]{:S(2)}) async-start(), calls=%async_computation.1 | async-start | bytes 1572864 | tf_op jit(solution)/shard_map/all_gather | solution.py:38
  7.9 159.7 %all-gather.9.cloned.1.call-start = ((), (), s32[]{:S(2)}) async-start(), calls=%async_computation.2 | async-start | bytes 8912896 | tf_op jit(solution)/shard_map/all_gather | solution.py:41
  8.7 352.1 %all-gather.11.cloned.1.call-start = ((), (), s32[]{:S(2)}) async-start(), calls=%async_computation.4 | async-start | bytes 17825792 | tf_op jit(solution)/shard_map/all_gather | solution.py:13
  11.7 541.6 %all-gather.13.cloned.1.call-start = ((), (), s32[]{:S(2)}) async-start(), calls=%async_computation.5 | async-start | bytes 17825792 | tf_op jit(solution)/shard_map/all_gather | solution.py:13
  176.1 4.1 copy-start.1
  180.3 719.7 %reduce-scatter.2.cloned.1.call-start = ((), (), s32[]{:S(2)}) async-start(), calls=%async_computation.3 | async-start | bytes 17825792 | tf_op jit(solution)/shard_map/reduce_scatter | solution.py:82
  182.3 1.3 copy-start.6
  360.9 2.2 copy-start.8
  372.1 2.1 copy-start.4
  375.0 2.0 copy-start.2
  375.0 2.7 copy-start.7
  579.3 2.4 copy-start.5
Sparse Core Ops, SparseCore 0:
  9.6 11.7 all-gather.6
  24.0 143.5 all-gather.8
  170.9 189.7 all-gather.10
  363.4 189.7 all-gather.12
  555.4 344.5 reduce-scatter.1
where the time goes:
time: 914 us; the launch traced here: 909 us
  waiting for transfers between devices  815 us (89%)
  matrix products  39.3 us (4%)
  other arithmetic  24.9 us (3%)
  local copies, waits for them, and re-layouts  14.8 us (2%)
  between operations  14 us (2%)
    all_gather x2, waiting for transfers between devices, entering(): gathered = lax.all_gather(part, axis)  345 us
    reduce_scatter x1, waiting for transfers between devices, per_device(): lax.psum_scatter(proj_term, 'seq', scatter_dimension=1, tiled=True)  313 us
    all_gather x1, waiting for transfers between devices, per_device(): lax.all_gather(proj_weight, 'seq', axis=1, tiled=True)  146 us
    add x15, other arithmetic, add_pair(): return earlier + later_one  22.6 us
  transfers between devices with their start and end apart: 5, of which 5 were waited for; matrix products, arithmetic and copies ran while one was open for 8% of the time, Pallas kernels for 0%

commit v1 on v0

--- a/solution.py
+++ b/solution.py
@@ -1,9 +1,424 @@
+import functools
+
 import jax
 import jax.numpy as jnp
+import numpy as np
 from jax import lax
+from jax.experimental import pallas as pl
+from jax.experimental.pallas import tpu as pltpu
 from jax.sharding import PartitionSpec as P
 
 DH = 128
+PLANE = 4
+PARTS = 2
+F32 = jnp.float32
+BF16 = jnp.bfloat16
+
+
+def dot(a, b, ca, cb):
+    return lax.dot_general(a, b, (((ca,), (cb,)), ((), ())), preferred_element_type=F32)
+
+
+def lanes(start, size):
+    return pl.ds(pl.multiple_of(start, DH), size)
+
+
+class Sems:
+    def __init__(self, send, recv):
+        self.send, self.recv, self.used = send, recv, 0
+
+    def take(self, count):
+        first = self.used
+        self.used += count
+        return first
+
+    def copy(self, i, src, dst, device):
+        return pltpu.make_async_remote_copy(
+            src_ref=src,
+            dst_ref=dst,
+            send_sem=self.send.at[i],
+            recv_sem=self.recv.at[i],
+            device_id=device,
+            device_id_type=pl.DeviceIdType.MESH,
+        )
+
+
+N_SEMS = 64
+
+
+def kernel(
+    depth, scale, proj_scale,
+    q, k, v, c, w,
+    gq, gk, gv, gp,
+    csend, cbuf, ct, wall, attn_s, aall, gsend, grecv, gown, gfull, pacc, pbf, precv,
+    gkpart, gvpart, st1, rv1, zs1, zr1, ps1, prior, st2, rv2, zs2, zr2, ps2, later, zacc,
+    send_sem, recv_sem,
+):
+    s, t = lax.axis_index("seq"), lax.axis_index("tp")
+    p, z = s % PLANE, s // PLANE
+    tok, width = q.shape
+    heads = width // DH
+    hq = heads // PLANE
+    half = c.shape[1] // PLANE
+    shard = w.shape[1]
+    sems = Sems(send_sem, recv_sem)
+    started = []
+
+    def peer(j):
+        if j == 0:
+            return p
+        if j == 1:
+            return p + 1 - 2 * (p % 2)
+        if j == 2:
+            return p + 2 - 4 * (p // 2)
+        return PLANE - 1 - p
+
+    def plane_dev(j, tt=None):
+        return (z * PLANE + peer(j), t if tt is None else tt)
+
+    def z_dev(zz):
+        return (zz * PLANE + p, t)
+
+    def up(j):
+        return (z + j) % depth
+
+    def down(j):
+        return (z + depth - j) % depth
+
+    barrier = pltpu.get_barrier_semaphore()
+    greet = [plane_dev(j) for j in range(1, PLANE)]
+    greet += [plane_dev(j, 1 - t) for j in range(PLANE)]
+    greet += [z_dev(up(j)) for j in range(1, depth)]
+    for dev in greet:
+        pl.semaphore_signal(barrier, inc=1, device_id=dev, device_id_type=pl.DeviceIdType.MESH)
+    pl.semaphore_wait(barrier, len(greet))
+
+    w_first = sems.take(depth)
+
+    def w_copy(j, slot):
+        return sems.copy(w_first + j, w, wall.at[:, lanes(slot * shard, shard)], z_dev(up(j)))
+
+    for j in range(1, depth):
+        cp = w_copy(j, z)
+        cp.start()
+        started.append(cp)
+
+    per = half // shard
+    for pp in range(PLANE):
+        for zl in range(per):
+            col = (zl * PLANE + pp) * shard
+            csend[pp, :, zl * shard : (zl + 1) * shard] = c[:, col : col + shard]
+    c_first = sems.take(2 * PLANE)
+
+    def c_copy(j, d, block, src_t):
+        return sems.copy(
+            c_first + 2 * j + d,
+            csend.at[peer(j)],
+            cbuf.at[block, :, lanes(src_t * half, half)],
+            plane_dev(j, t if d == 0 else 1 - t),
+        )
+
+    def scan_states(a, b, st):
+        def one(h, _):
+            cols = lanes(h * DH, DH)
+            st[h // hq, h % hq] = dot(a[:, cols], b[:, cols], 0, 0).astype(BF16)
+            return 0
+
+        lax.fori_loop(0, heads, one, 0)
+
+    def scan_start(st, rv):
+        first = sems.take(PLANE)
+
+        def cp(j, slot):
+            return sems.copy(first + j, st.at[peer(j)], rv.at[slot], plane_dev(j))
+
+        for j in range(1, PLANE):
+            x = cp(j, p)
+            x.start()
+            started.append(x)
+        rv[p] = st[p]
+        return cp
+
+    def scan_depth(cp, rv, zs, zr, reverse):
+        for j in range(1, PLANE):
+            cp(j, peer(j)).wait_recv()
+        total = rv[0].astype(F32)
+        for pp in range(1, PLANE):
+            total = total + rv[pp].astype(F32)
+        zs[...] = total.astype(BF16)
+        first = sems.take(depth)
+
+        def zcp(j, slot):
+            return sems.copy(first + j, zs, zr.at[slot], z_dev(down(j) if reverse else up(j)))
+
+        for j in range(1, depth):
+            @pl.when(z - j >= 0 if reverse else z + j < depth)
+            def _():
+                zcp(j, z).start()
+        return zcp
+
+    def scan_spread(zcp, rv, zr, ps, out, reverse):
+        zacc[...] = jnp.zeros_like(zacc)
+        for j in range(1, depth):
+            @pl.when(z + j < depth if reverse else z - j >= 0)
+            def _():
+                src = up(j) if reverse else down(j)
+                zcp(j, src).wait_recv()
+                zacc[...] += zr[src].astype(F32)
+
+        def one(i, _):
+            run = zacc[i]
+            order = range(PLANE)
+            for pp in reversed(order) if reverse else order:
+                ps[pp, i] = run.astype(BF16)
+                run = run + rv[pp, i].astype(F32)
+            return 0
+
+        lax.fori_loop(0, hq, one, 0)
+        first = sems.take(PLANE)
+
+        def cp(j, slot):
+            return sems.copy(first + j, ps.at[peer(j)], out.at[slot], plane_dev(j))
+
+        for j in range(1, PLANE):
+            x = cp(j, p)
+            x.start()
+            started.append(x)
+        out[p] = ps[p]
+        return cp
+
+    def scan_depth_sent(zcp, reverse):
+        for j in range(1, depth):
+            @pl.when(z - j >= 0 if reverse else z + j < depth)
+            def _():
+                zcp(j, z).wait_send()
+
+    scan_states(k, v, st1)
+    kv_cp = scan_start(st1, rv1)
+
+    for j in range(PLANE):
+        for d in range(2):
+            if j or d:
+                cp = c_copy(j, d, p, t)
+                cp.start()
+                started.append(cp)
+    cbuf[p, :, lanes(t * half, half)] = csend[p]
+    wall[:, lanes(z * shard, shard)] = w[...]
+
+    causal = lax.broadcasted_iota(jnp.int32, (tok, tok), 0) >= lax.broadcasted_iota(
+        jnp.int32, (tok, tok), 1
+    )
+
+    def attn_head(h, _):
+        cols = lanes(h * DH, DH)
+        attn_s[h] = jnp.where(causal, dot(q[:, cols], k[:, cols], 1, 1), 0.0).astype(BF16)
+        return 0
+
+    lax.fori_loop(0, heads // 2, attn_head, 0)
+    kv_z = scan_depth(kv_cp, rv1, zs1, zr1, False)
+    lax.fori_loop(heads // 2, heads, attn_head, 0)
+    kv_prior = scan_spread(kv_z, rv1, zr1, ps1, prior, False)
+    for j in range(PLANE):
+        for d in range(2):
+            if j or d:
+                c_copy(j, d, peer(j), t if d == 0 else 1 - t).wait_recv()
+    for pp in range(PLANE):
+        ct[:, pp * tok : (pp + 1) * tok] = cbuf[pp].T
+    for j in range(1, PLANE):
+        kv_prior(j, peer(j)).wait_recv()
+
+    def out_head(h, _):
+        cols = lanes(h * DH, DH)
+        a = dot(attn_s[h], v[:, cols], 1, 0) + dot(q[:, cols], prior[h // hq, h % hq], 1, 0)
+        aall[p, :, cols] = (scale * a).astype(BF16)
+        return 0
+
+    piece = width // PARTS
+    a_first = sems.take(PARTS * PLANE)
+
+    def a_copy(part, j, block):
+        cols = pl.ds(part * piece, piece)
+        return sems.copy(
+            a_first + part * PLANE + j, aall.at[p, :, cols], aall.at[block, :, cols], plane_dev(j)
+        )
+
+    for part in range(PARTS):
+        lax.fori_loop(part * heads // PARTS, (part + 1) * heads // PARTS, out_head, 0)
+        for j in range(1, PLANE):
+            cp = a_copy(part, j, p)
+            cp.start()
+            started.append(cp)
+
+    for j in range(1, depth):
+        w_copy(j, down(j)).wait_recv()
+    step = 4 * DH
+    g_first = sems.take(PLANE)
+
+    def g_copy(j):
+        return sems.copy(g_first + j, gsend.at[j - 1], grecv.at[j - 1], plane_dev(j))
+
+    for j in (3, 1, 2, 0):
+        mine = peer(j)
+
+        def g_chunk(i, _):
+            cols = lanes(i * step, step)
+            rows = pl.ds(pl.multiple_of(i * step, step), step)
+            r = dot(cbuf[mine], wall[rows, :], 1, 1)
+            if j:
+                gsend[j - 1, :, cols] = r.astype(BF16)
+            else:
+                gown[:, cols] = r
+            return 0
+
+        lax.fori_loop(0, width // step, g_chunk, 0)
+        if j:
+            cp = g_copy(j)
+            cp.start()
+            started.append(cp)
+
+    p_first = sems.take(PARTS * depth)
+
+    def p_copy(part, j, slot):
+        cols = pl.ds(part * piece, piece)
+        return sems.copy(
+            p_first + part * depth + j,
+            pbf.at[up(j), :, cols],
+            precv.at[slot, :, cols],
+            z_dev(up(j)),
+        )
+
+    def p_chunk(i, _):
+        cols = lanes(i * step, step)
+        r = dot(ct[...], aall[:, :, cols].reshape(PLANE * tok, step), 1, 0)
+        r = r.reshape(depth, shard, step)
+        pacc[...] = r
+        pbf[:, :, cols] = r.astype(BF16)
+        gp[:, cols] = pacc[z]
+        return 0
+
+    for part in range(PARTS):
+        for j in range(1, PLANE):
+            a_copy(part, j, peer(j)).wait_recv()
+        lax.fori_loop(part * piece // step, (part + 1) * piece // step, p_chunk, 0)
+        for j in range(1, depth):
+            cp = p_copy(part, j, z)
+            cp.start()
+            started.append(cp)
+
+    for j in (1, 2, 3):
+        g_copy(j).wait_recv()
+
+    def g_sum(i, _):
+        cols = lanes(i * step, step)
+        r = gown[:, cols]
+        for j in range(PLANE - 1):
+            r = r + grecv[j, :, cols].astype(F32)
+        gfull[:, cols] = r.astype(BF16)
+        return 0
+
+    lax.fori_loop(0, width // step, g_sum, 0)
+    scan_states(q, gfull, st2)
+    qg_cp = scan_start(st2, rv2)
+
+    def inner_head(h, _):
+        cols = lanes(h * DH, DH)
+        gh = gfull[:, cols]
+        back = jnp.where(causal, dot(gh, v[:, cols], 1, 1), 0.0).astype(BF16)
+        dq = dot(back, k[:, cols], 1, 0) + dot(gh, prior[h // hq, h % hq], 1, 1)
+        gq[:, cols] = (scale * dq).astype(BF16)
+        gkpart[:, cols] = dot(back, q[:, cols], 0, 0)
+        gvpart[:, cols] = dot(attn_s[h], gh, 0, 0)
+        return 0
+
+    lax.fori_loop(0, heads // 2, inner_head, 0)
+    qg_z = scan_depth(qg_cp, rv2, zs2, zr2, True)
+    lax.fori_loop(heads // 2, heads, inner_head, 0)
+    qg_later = scan_spread(qg_z, rv2, zr2, ps2, later, True)
+
+    for part in range(PARTS):
+        for j in range(1, depth):
+            p_copy(part, j, down(j)).wait_recv()
+
+    def p_sum(i, _):
+        cols = lanes(i * step, step)
+        r = gp[:, cols]
+        for j in range(1, depth):
+            r = r + precv[down(j), :, cols].astype(F32)
+        gp[:, cols] = r * proj_scale
+        return 0
+
+    lax.fori_loop(0, width // step, p_sum, 0)
+    for j in range(1, PLANE):
+        qg_later(j, peer(j)).wait_recv()
+
+    def last_head(h, _):
+        cols = lanes(h * DH, DH)
+        la = later[h // hq, h % hq]
+        gk[:, cols] = (scale * (gkpart[:, cols] + dot(v[:, cols], la, 1, 1))).astype(BF16)
+        gv[:, cols] = (scale * (gvpart[:, cols] + dot(k[:, cols], la, 1, 0))).astype(BF16)
+        return 0
+
+    lax.fori_loop(0, heads, last_head, 0)
+
+    for cp in started:
+        cp.wait_send()
+    scan_depth_sent(kv_z, False)
+    scan_depth_sent(qg_z, True)
+
+
+def fused(n_seq, queries, keys, values, out_cotangent, proj_weight):
+    tok, width = queries.shape
+    heads = width // DH
+    hq = heads // PLANE
+    depth = n_seq // PLANE
+    half = out_cotangent.shape[1] // PLANE
+    shard = proj_weight.shape[1]
+    scale = np.float32(1.0) / np.sqrt(np.float32(DH * tok * n_seq))
+    proj_scale = np.float32(1.0) / np.sqrt(np.float32(tok * n_seq))
+    bf = lambda *dims: pltpu.VMEM(dims, BF16)
+    f32 = lambda *dims: pltpu.VMEM(dims, F32)
+    scan = [
+        bf(PLANE, hq, DH, DH),
+        bf(PLANE, hq, DH, DH),
+        bf(hq, DH, DH),
+        bf(depth, hq, DH, DH),
+        bf(PLANE, hq, DH, DH),
+        bf(PLANE, hq, DH, DH),
+    ]
+    vmem = pl.BlockSpec(memory_space=pltpu.VMEM)
+    grad = jax.ShapeDtypeStruct((tok, width), BF16)
+    gq, gk, gv, gp = pl.pallas_call(
+        functools.partial(kernel, depth, scale, proj_scale),
+        out_shape=(grad, grad, grad, jax.ShapeDtypeStruct((shard, width), F32)),
+        in_specs=[vmem] * 5,
+        out_specs=(vmem,) * 4,
+        scratch_shapes=[
+            bf(PLANE, tok, half),
+            bf(PLANE, tok, 2 * half),
+            bf(2 * half, PLANE * tok),
+            bf(width, 2 * half),
+            bf(heads, tok, tok),
+            bf(PLANE, tok, width),
+            bf(PLANE - 1, tok, width),
+            bf(PLANE - 1, tok, width),
+            f32(tok, width),
+            bf(tok, width),
+            f32(depth, shard, 4 * DH),
+            bf(depth, shard, width),
+            bf(depth, shard, width),
+            f32(tok, width),
+            f32(tok, width),
+            *scan,
+            *scan,
+            f32(hq, DH, DH),
+            pltpu.SemaphoreType.DMA((N_SEMS,)),
+            pltpu.SemaphoreType.DMA((N_SEMS,)),
+        ],
+        compiler_params=pltpu.CompilerParams(
+            collective_id=0, has_side_effects=True, vmem_limit_bytes=58 * 1024 * 1024
+        ),
+    )(queries, keys, values, out_cotangent, proj_weight)
+    return gq, gk, gv, gp.T
 
 
 def entering(part, axis, combine, identity, reverse):
@@ -24,7 +439,7 @@
     return earlier + later_one
 
 
-def per_device(queries, keys, values, out_cotangent, proj_weight):
+def gathered(queries, keys, values, out_cotangent, proj_weight):
     tok = queries.shape[0]
     heads = queries.shape[1] // DH
     seq_count = lax.axis_size("seq")
@@ -90,9 +505,17 @@
     )
 
 
+def per_device(n_seq, n_tp, *args):
+    width, shard = args[0].shape[1], args[4].shape[1]
+    groups = n_seq % (2 * PLANE) == 0 and n_tp == 2
+    if groups and shard % DH == 0 and width % (4 * DH * PARTS) == 0:
+        return fused(n_seq, *args)
+    return gathered(*args)
+
+
 def solution(mesh):
     return jax.shard_map(
-        per_device,
+        functools.partial(per_device, mesh.shape["seq"], mesh.shape["tp"]),
         mesh=mesh,
         in_specs=(P("seq", "tp"), P("seq", "tp"), P("seq", "tp"), P("seq", "tp"), P("tp", "seq")),
         out_specs=(P("seq", "tp"), P("seq", "tp"), P("seq", "tp"), P("tp", "seq")),

time: 914 us -> 203 us (0.22)
  waiting for transfers between devices: 815 us -> 0 us
  Pallas kernels: 0 us -> 196 us
  matrix products: 39.3 us -> 0 us
  other arithmetic: 24.9 us -> 0 us
  between operations: 14 us -> 0.65 us
    all_gather x4 -> x0, waiting for transfers between devices: 501 us -> none  [the longest x2 345 us: entering(): gathered = lax.all_gather(part, axis)]
    reduce_scatter x1 -> x0, waiting for transfers between devices: 313 us -> none  [per_device(): lax.psum_scatter(proj_term, 'seq', scatter_dimension=1, tiled=True)]
    pallas_call x0 -> x1, Pallas kernels: none -> 196 us  [fused(): pl.pallas_call(functools.partial(kernel, depth, scale, proj_scale), out_s...]
    dot_general x14 -> x0, matrix products: 39.3 us -> none  [the longest x1 8.96 us: per_device(): lax.dot_general(out_flat, full_cot, (((0,), (0,)), ((), ())), preferred_e...]
    add x15 -> x0, other arithmetic: 22.6 us -> none  [add_pair(): return earlier + later_one]
  transfers between devices with their start and end apart: 5 -> 0, of which waited for: 5 -> 0; matrix products, arithmetic and copies ran while one was open for 8% -> 0% of each run, Pallas kernels for 0% -> 0%
where the time goes in v1:
time: 203 us
  Pallas kernels  196 us (97%)
  local copies, waits for them, and re-layouts  6.8 us (3%)
    pallas_call x1, Pallas kernels, fused(): pl.pallas_call(functools.partial(kernel, depth, scale, proj_scale), out_s...  196 us
    unnamed x10, local copies, waits for them, and re-layouts  6.8 us

profile of v1, /device:TPU:0, one launch (start us, length us, event | category | flops | bytes accessed | tf_op | source)
XLA Modules:
  0.0 203.1 jit_solution(16059472702228391358)
XLA Ops:
  0.6 195.6 %shard_map.84 = (bf16[256,2048]{1,0:T(8,128)(2,1)}, bf16[256,2048]{1,0:T(8,128)(2,1)}, bf16[256,2048]{1,0:T(8,128)(2,1)}, f32[128,2048]{1,0:T(8,128)}) custom-call(bf16[256,2048]{1,0:T(8,128)(2,1)} %q.1, bf16[256,2048]{1,0:T(8,128)(2,1)} %k.1, bf16[256,2048]{1,0:T(8,128)(2,1)} %v.1, bf16[256,1024]{1,0:T(8,128)(2,1)} %c.1, bf16[2048,128]{1,0:T(8,128)(2,1)} %w.1), custom_call_target="tpu_custom_call" | custom-call | tf_op jit(solution)/shard_map/pallas_call | solution.py:390
  196.3 0.0 copy-start.2
  196.3 2.6 %copy.9 = f32[2048,128]{1,0:T(8,128)} copy(f32[2048,128]{0,1:T(8,128)} %bitcast.1) | data formatting | bytes 2097152
  198.9 0.0 copy-done.2
  198.9 0.0 copy-start.1
  198.9 1.0 copy.13
  199.9 0.6 copy-done.1
  200.5 0.0 copy-start
  200.5 1.0 copy.14
  201.5 0.6 copy-done
  202.1 1.0 copy.15
Async XLA Ops:
  196.3 2.6 %copy-start.2 = (bf16[256,2048]{1,0:T(8,128)(2,1)S(1)}, bf16[256,2048]{1,0:T(8,128)(2,1)}, u32[]{:S(2)}) copy-start(bf16[256,2048]{1,0:T(8,128)(2,1)} %get-tuple-element.20) | copy-start | bytes 3145732
  198.9 1.6 copy-start.1
  200.5 1.6 copy-start

commit v2 on v1

--- a/solution.py
+++ b/solution.py
@@ -10,7 +10,7 @@
 
 DH = 128
 PLANE = 4
-PARTS = 2
+PARTS = 4
 F32 = jnp.float32
 BF16 = jnp.bfloat16
 
@@ -43,14 +43,14 @@
         )
 
 
-N_SEMS = 64
+N_SEMS = 128
 
 
 def kernel(
     depth, scale, proj_scale,
     q, k, v, c, w,
     gq, gk, gv, gp,
-    csend, cbuf, ct, wall, attn_s, aall, gsend, grecv, gown, gfull, pacc, pbf, precv,
+    csend, cbuf, ct, wall, attn_s, aall, gs1, gr1, gkeep, gs2, gr2, gfull, pacc, pown, pbf, precv,
     gkpart, gvpart, st1, rv1, zs1, zr1, ps1, prior, st2, rv2, zs2, zr2, ps2, later, zacc,
     send_sem, recv_sem,
 ):
@@ -58,7 +58,7 @@
     p, z = s % PLANE, s // PLANE
     tok, width = q.shape
     heads = width // DH
-    hq = heads // PLANE
+    hq = heads // (2 * PLANE)
     half = c.shape[1] // PLANE
     shard = w.shape[1]
     sems = Sems(send_sem, recv_sem)
@@ -91,17 +91,28 @@
     greet += [z_dev(up(j)) for j in range(1, depth)]
     for dev in greet:
         pl.semaphore_signal(barrier, inc=1, device_id=dev, device_id_type=pl.DeviceIdType.MESH)
-    pl.semaphore_wait(barrier, len(greet))
-
-    w_first = sems.take(depth)
-
-    def w_copy(j, slot):
-        return sems.copy(w_first + j, w, wall.at[:, lanes(slot * shard, shard)], z_dev(up(j)))
-
-    for j in range(1, depth):
-        cp = w_copy(j, z)
-        cp.start()
-        started.append(cp)
+
+    w_first = sems.take(3 * depth)
+    w_cuts = (0, width // 4, width // 2, width)
+
+    def w_copy(part, j, slot):
+        rows = pl.ds(w_cuts[part], w_cuts[part + 1] - w_cuts[part])
+        return sems.copy(
+            w_first + part * depth + j,
+            w.at[rows, :],
+            wall.at[rows, lanes(slot * shard, shard)],
+            z_dev(up(j)),
+        )
+
+    def w_send(part):
+        for j in range(1, depth):
+            cp = w_copy(part, j, z)
+            cp.start()
+            started.append(cp)
+
+    def w_wait(part):
+        for j in range(1, depth):
+            w_copy(part, j, down(j)).wait_recv()
 
     per = half // shard
     for pp in range(PLANE):
@@ -110,21 +121,34 @@
             csend[pp, :, zl * shard : (zl + 1) * shard] = c[:, col : col + shard]
     c_first = sems.take(2 * PLANE)
 
-    def c_copy(j, d, block, src_t):
+    def c_copy(j, block):
         return sems.copy(
-            c_first + 2 * j + d,
-            csend.at[peer(j)],
-            cbuf.at[block, :, lanes(src_t * half, half)],
-            plane_dev(j, t if d == 0 else 1 - t),
-        )
-
-    def scan_states(a, b, st):
-        def one(h, _):
+            c_first + j, csend.at[peer(j)], cbuf.at[block, :, lanes(t * half, half)], plane_dev(j)
+        )
+
+    def c_pass(j, src_t):
+        there = cbuf.at[peer(j), :, lanes(src_t * half, half)]
+        return sems.copy(c_first + PLANE + j, there, there, plane_dev(0, 1 - t))
+
+    def each_head(lo, hi, one):
+        group = heads // 4
+
+        def some(i, _):
+            for u in range(group):
+                one(lo + i * group + u)
+            return 0
+
+        lax.fori_loop(0, (hi - lo) // group, some, 0)
+
+    def of_head(h):
+        return h // (PLANE * hq), h // hq % PLANE, h % hq
+
+    def scan_states(a, b, st, hi):
+        def one(h):
             cols = lanes(h * DH, DH)
-            st[h // hq, h % hq] = dot(a[:, cols], b[:, cols], 0, 0).astype(BF16)
-            return 0
-
-        lax.fori_loop(0, heads, one, 0)
+            st[h // hq % PLANE, h % hq] = dot(a[:, cols], b[:, cols], 0, 0).astype(BF16)
+
+        each_head(hi * heads // 2, (hi + 1) * heads // 2, one)
 
     def scan_start(st, rv):
         first = sems.take(PLANE)
@@ -193,93 +217,135 @@
             def _():
                 zcp(j, z).wait_send()
 
-    scan_states(k, v, st1)
-    kv_cp = scan_start(st1, rv1)
-
-    for j in range(PLANE):
-        for d in range(2):
-            if j or d:
-                cp = c_copy(j, d, p, t)
+    kv_cp, kv_z, kv_prior = {}, {}, {}
+    scan_states(k, v, st1.at[0], 0)
+    pl.semaphore_wait(barrier, len(greet))
+    kv_cp[0] = scan_start(st1.at[0], rv1.at[0])
+    w_send(0)
+    scan_states(k, v, st1.at[1], 1)
+    kv_cp[1] = scan_start(st1.at[1], rv1.at[1])
+    cbuf[p, :, lanes(t * half, half)] = csend[p]
+    for j in range(1, PLANE):
+        cp = c_copy(j, p)
+        cp.start()
+        started.append(cp)
+    cp = c_pass(0, t)
+    cp.start()
+    started.append(cp)
+    wall[:, lanes(z * shard, shard)] = w[...]
+
+    causal = lax.broadcasted_iota(jnp.int32, (tok, tok), 0) >= lax.broadcasted_iota(
+        jnp.int32, (tok, tok), 1
+    )
+
+    def attn_head(h):
+        cols = lanes(h * DH, DH)
+        attn_s[h] = jnp.where(causal, dot(q[:, cols], k[:, cols], 1, 1), 0.0).astype(BF16)
+
+    each_head(0, heads // 2, attn_head)
+    for hi in range(2):
+        kv_z[hi] = scan_depth(kv_cp[hi], rv1.at[hi], zs1.at[hi], zr1.at[hi], False)
+    w_send(1)
+    w_send(2)
+    each_head(heads // 2, heads, attn_head)
+    for j in range(1, PLANE):
+        c_copy(j, peer(j)).wait_recv()
+        cp = c_pass(j, t)
+        cp.start()
+        started.append(cp)
+
+    def out_head(h):
+        cols = lanes(h * DH, DH)
+        a = dot(attn_s[h], v[:, cols], 1, 0) + dot(q[:, cols], prior[of_head(h)], 1, 0)
+        aall[p, :, cols] = (scale * a).astype(BF16)
+
+    step = width // PARTS
+    a_first = sems.take(PARTS * PLANE)
+
+    def a_copy(part, j, block):
+        cols = pl.ds(part * step, step)
+        return sems.copy(
+            a_first + part * PLANE + j, aall.at[p, :, cols], aall.at[block, :, cols], plane_dev(j)
+        )
+
+    def a_pass(part, block):
+        cols = pl.ds(part * step, step)
+        via = 1 + part % 2
+        return sems.copy(
+            a_first + part * PLANE + 3,
+            aall.at[peer(via), :, cols],
+            aall.at[block, :, cols],
+            plane_dev(3 - via),
+        )
+
+    for hi in range(2):
+        kv_prior[hi] = scan_spread(
+            kv_z[hi], rv1.at[hi], zr1.at[hi], ps1.at[hi], prior.at[hi], False
+        )
+        for j in range(1, PLANE):
+            kv_prior[hi](j, peer(j)).wait_recv()
+        for part in (2 * hi, 2 * hi + 1):
+            each_head(part * heads // PARTS, (part + 1) * heads // PARTS, out_head)
+            for j in (1, 2):
+                cp = a_copy(part, j, p)
                 cp.start()
                 started.append(cp)
-    cbuf[p, :, lanes(t * half, half)] = csend[p]
-    wall[:, lanes(z * shard, shard)] = w[...]
-
-    causal = lax.broadcasted_iota(jnp.int32, (tok, tok), 0) >= lax.broadcasted_iota(
-        jnp.int32, (tok, tok), 1
-    )
-
-    def attn_head(h, _):
-        cols = lanes(h * DH, DH)
-        attn_s[h] = jnp.where(causal, dot(q[:, cols], k[:, cols], 1, 1), 0.0).astype(BF16)
-        return 0
-
-    lax.fori_loop(0, heads // 2, attn_head, 0)
-    kv_z = scan_depth(kv_cp, rv1, zs1, zr1, False)
-    lax.fori_loop(heads // 2, heads, attn_head, 0)
-    kv_prior = scan_spread(kv_z, rv1, zr1, ps1, prior, False)
     for j in range(PLANE):
-        for d in range(2):
-            if j or d:
-                c_copy(j, d, peer(j), t if d == 0 else 1 - t).wait_recv()
+        c_pass(j, 1 - t).wait_recv()
     for pp in range(PLANE):
         ct[:, pp * tok : (pp + 1) * tok] = cbuf[pp].T
-    for j in range(1, PLANE):
-        kv_prior(j, peer(j)).wait_recv()
-
-    def out_head(h, _):
-        cols = lanes(h * DH, DH)
-        a = dot(attn_s[h], v[:, cols], 1, 0) + dot(q[:, cols], prior[h // hq, h % hq], 1, 0)
-        aall[p, :, cols] = (scale * a).astype(BF16)
-        return 0
-
-    piece = width // PARTS
-    a_first = sems.take(PARTS * PLANE)
-
-    def a_copy(part, j, block):
-        cols = pl.ds(part * piece, piece)
+    for part in range(PARTS):
+        via = 1 + part % 2
+        a_copy(part, via, peer(via)).wait_recv()
+        cp = a_pass(part, peer(via))
+        cp.start()
+        started.append(cp)
+
+    def g_block(part, block, out):
+        rows = pl.ds(part * step, step)
+        out[...] = dot(cbuf[block], wall[rows, :], 1, 1).astype(out.dtype)
+
+    g_first = sems.take(3 * PARTS)
+
+    def g_copy1(part, b):
         return sems.copy(
-            a_first + part * PLANE + j, aall.at[p, :, cols], aall.at[block, :, cols], plane_dev(j)
-        )
-
-    for part in range(PARTS):
-        lax.fori_loop(part * heads // PARTS, (part + 1) * heads // PARTS, out_head, 0)
-        for j in range(1, PLANE):
-            cp = a_copy(part, j, p)
+            g_first + 3 * part + b, gs1.at[part, b], gr1.at[part, b], plane_dev(1 + part % 2)
+        )
+
+    def g_copy2(part):
+        return sems.copy(g_first + 3 * part + 2, gs2.at[part], gr2.at[part], plane_dev(2 - part % 2))
+
+    def g_first_step(hi):
+        both = (2 * hi, 2 * hi + 1)
+        for b in (1, 0):
+            for part in both:
+                g_block(part, peer(3 if b else 1 + part % 2), gs1.at[part, b])
+                cp = g_copy1(part, b)
+                cp.start()
+                started.append(cp)
+        for b in (1, 0):
+            for part in both:
+                g_block(part, peer(2 - part % 2) if b else p, gkeep.at[part, b])
+
+    def g_second_step(hi):
+        for part in (2 * hi, 2 * hi + 1):
+            g_copy1(part, 1).wait_recv()
+            gs2[part] = (gkeep[part, 1] + gr1[part, 1].astype(F32)).astype(BF16)
+            cp = g_copy2(part)
             cp.start()
             started.append(cp)
 
-    for j in range(1, depth):
-        w_copy(j, down(j)).wait_recv()
-    step = 4 * DH
-    g_first = sems.take(PLANE)
-
-    def g_copy(j):
-        return sems.copy(g_first + j, gsend.at[j - 1], grecv.at[j - 1], plane_dev(j))
-
-    for j in (3, 1, 2, 0):
-        mine = peer(j)
-
-        def g_chunk(i, _):
-            cols = lanes(i * step, step)
-            rows = pl.ds(pl.multiple_of(i * step, step), step)
-            r = dot(cbuf[mine], wall[rows, :], 1, 1)
-            if j:
-                gsend[j - 1, :, cols] = r.astype(BF16)
-            else:
-                gown[:, cols] = r
-            return 0
-
-        lax.fori_loop(0, width // step, g_chunk, 0)
-        if j:
-            cp = g_copy(j)
-            cp.start()
-            started.append(cp)
+    def g_final(hi):
+        for part in (2 * hi, 2 * hi + 1):
+            g_copy1(part, 0).wait_recv()
+            g_copy2(part).wait_recv()
+            total = gkeep[part, 0] + gr1[part, 0].astype(F32) + gr2[part].astype(F32)
+            gfull[:, part * step : (part + 1) * step] = total.astype(BF16)
 
     p_first = sems.take(PARTS * depth)
 
     def p_copy(part, j, slot):
-        cols = pl.ds(part * piece, piece)
+        cols = pl.ds(part * step, step)
         return sems.copy(
             p_first + part * depth + j,
             pbf.at[up(j), :, cols],
@@ -287,89 +353,92 @@
             z_dev(up(j)),
         )
 
-    def p_chunk(i, _):
-        cols = lanes(i * step, step)
+    def p_part(part):
+        via = 1 + part % 2
+        a_copy(part, 3 - via, peer(3 - via)).wait_recv()
+        a_pass(part, peer(3)).wait_recv()
+        cols = pl.ds(part * step, step)
         r = dot(ct[...], aall[:, :, cols].reshape(PLANE * tok, step), 1, 0)
         r = r.reshape(depth, shard, step)
         pacc[...] = r
         pbf[:, :, cols] = r.astype(BF16)
-        gp[:, cols] = pacc[z]
-        return 0
-
-    for part in range(PARTS):
-        for j in range(1, PLANE):
-            a_copy(part, j, peer(j)).wait_recv()
-        lax.fori_loop(part * piece // step, (part + 1) * piece // step, p_chunk, 0)
+        pown[:, cols] = pacc[z]
         for j in range(1, depth):
             cp = p_copy(part, j, z)
             cp.start()
             started.append(cp)
 
-    for j in (1, 2, 3):
-        g_copy(j).wait_recv()
-
-    def g_sum(i, _):
-        cols = lanes(i * step, step)
-        r = gown[:, cols]
-        for j in range(PLANE - 1):
-            r = r + grecv[j, :, cols].astype(F32)
-        gfull[:, cols] = r.astype(BF16)
-        return 0
-
-    lax.fori_loop(0, width // step, g_sum, 0)
-    scan_states(q, gfull, st2)
-    qg_cp = scan_start(st2, rv2)
-
-    def inner_head(h, _):
+    w_wait(0)
+    w_wait(1)
+    g_first_step(0)
+    p_part(0)
+    p_part(1)
+    g_second_step(0)
+    w_wait(2)
+    g_first_step(1)
+    p_part(2)
+    p_part(3)
+
+    qg_cp, qg_z, qg_later = {}, {}, {}
+    g_final(0)
+    scan_states(q, gfull, st2.at[0], 0)
+    qg_cp[0] = scan_start(st2.at[0], rv2.at[0])
+    g_second_step(1)
+
+    def inner_head(h):
         cols = lanes(h * DH, DH)
         gh = gfull[:, cols]
         back = jnp.where(causal, dot(gh, v[:, cols], 1, 1), 0.0).astype(BF16)
-        dq = dot(back, k[:, cols], 1, 0) + dot(gh, prior[h // hq, h % hq], 1, 1)
+        dq = dot(back, k[:, cols], 1, 0) + dot(gh, prior[of_head(h)], 1, 1)
         gq[:, cols] = (scale * dq).astype(BF16)
         gkpart[:, cols] = dot(back, q[:, cols], 0, 0)
         gvpart[:, cols] = dot(attn_s[h], gh, 0, 0)
-        return 0
-
-    lax.fori_loop(0, heads // 2, inner_head, 0)
-    qg_z = scan_depth(qg_cp, rv2, zs2, zr2, True)
-    lax.fori_loop(heads // 2, heads, inner_head, 0)
-    qg_later = scan_spread(qg_z, rv2, zr2, ps2, later, True)
+
+    each_head(0, heads // 2, inner_head)
+    qg_z[0] = scan_depth(qg_cp[0], rv2.at[0], zs2.at[0], zr2.at[0], True)
+    g_final(1)
+    scan_states(q, gfull, st2.at[1], 1)
+    qg_cp[1] = scan_start(st2.at[1], rv2.at[1])
+    each_head(heads // 2, heads, inner_head)
+    qg_z[1] = scan_depth(qg_cp[1], rv2.at[1], zs2.at[1], zr2.at[1], True)
+    qg_later[0] = scan_spread(qg_z[0], rv2.at[0], zr2.at[0], ps2.at[0], later.at[0], True)
 
     for part in range(PARTS):
         for j in range(1, depth):
             p_copy(part, j, down(j)).wait_recv()
 
-    def p_sum(i, _):
-        cols = lanes(i * step, step)
-        r = gp[:, cols]
+    for part in range(PARTS):
+        cols = pl.ds(part * step, step)
+        r = pown[:, cols]
         for j in range(1, depth):
             r = r + precv[down(j), :, cols].astype(F32)
-        gp[:, cols] = r * proj_scale
-        return 0
-
-    lax.fori_loop(0, width // step, p_sum, 0)
-    for j in range(1, PLANE):
-        qg_later(j, peer(j)).wait_recv()
-
-    def last_head(h, _):
+        gp[cols, :] = (r * proj_scale).T
+
+    def last_head(h):
         cols = lanes(h * DH, DH)
-        la = later[h // hq, h % hq]
+        la = later[of_head(h)]
         gk[:, cols] = (scale * (gkpart[:, cols] + dot(v[:, cols], la, 1, 1))).astype(BF16)
         gv[:, cols] = (scale * (gvpart[:, cols] + dot(k[:, cols], la, 1, 0))).astype(BF16)
-        return 0
-
-    lax.fori_loop(0, heads, last_head, 0)
+
+    for j in range(1, PLANE):
+        qg_later[0](j, peer(j)).wait_recv()
+    each_head(0, heads // 2, last_head)
+    qg_later[1] = scan_spread(qg_z[1], rv2.at[1], zr2.at[1], ps2.at[1], later.at[1], True)
+    for j in range(1, PLANE):
+        qg_later[1](j, peer(j)).wait_recv()
+    each_head(heads // 2, heads, last_head)
 
     for cp in started:
         cp.wait_send()
-    scan_depth_sent(kv_z, False)
-    scan_depth_sent(qg_z, True)
+    for hi in range(2):
+        scan_depth_sent(kv_z[hi], False)
+        scan_depth_sent(qg_z[hi], True)
 
 
 def fused(n_seq, queries, keys, values, out_cotangent, proj_weight):
     tok, width = queries.shape
     heads = width // DH
-    hq = heads // PLANE
+    hq = heads // (2 * PLANE)
     depth = n_seq // PLANE
     half = out_cotangent.shape[1] // PLANE
     shard = proj_weight.shape[1]
@@ -378,18 +447,18 @@
     bf = lambda *dims: pltpu.VMEM(dims, BF16)
     f32 = lambda *dims: pltpu.VMEM(dims, F32)
     scan = [
-        bf(PLANE, hq, DH, DH),
-        bf(PLANE, hq, DH, DH),
-        bf(hq, DH, DH),
-        bf(depth, hq, DH, DH),
-        bf(PLANE, hq, DH, DH),
-        bf(PLANE, hq, DH, DH),
+        bf(2, PLANE, hq, DH, DH),
+        bf(2, PLANE, hq, DH, DH),
+        bf(2, hq, DH, DH),
+        bf(2, depth, hq, DH, DH),
+        bf(2, PLANE, hq, DH, DH),
+        bf(2, PLANE, hq, DH, DH),
     ]
     vmem = pl.BlockSpec(memory_space=pltpu.VMEM)
     grad = jax.ShapeDtypeStruct((tok, width), BF16)
-    gq, gk, gv, gp = pl.pallas_call(
+    return pl.pallas_call(
         functools.partial(kernel, depth, scale, proj_scale),
-        out_shape=(grad, grad, grad, jax.ShapeDtypeStruct((shard, width), F32)),
+        out_shape=(grad, grad, grad, jax.ShapeDtypeStruct((width, shard), F32)),
         in_specs=[vmem] * 5,
         out_specs=(vmem,) * 4,
         scratch_shapes=[
@@ -399,11 +468,14 @@
             bf(width, 2 * half),
             bf(heads, tok, tok),
             bf(PLANE, tok, width),
-            bf(PLANE - 1, tok, width),
-            bf(PLANE - 1, tok, width),
-            f32(tok, width),
+            bf(PARTS, 2, tok, width // PARTS),
+            bf(PARTS, 2, tok, width // PARTS),
+            f32(PARTS, 2, tok, width // PARTS),
+            bf(PARTS, tok, width // PARTS),
+            bf(PARTS, tok, width // PARTS),
             bf(tok, width),
-            f32(depth, shard, 4 * DH),
+            f32(depth, shard, width // PARTS),
+            f32(shard, width),
             bf(depth, shard, width),
             bf(depth, shard, width),
             f32(tok, width),
@@ -418,7 +490,6 @@
             collective_id=0, has_side_effects=True, vmem_limit_bytes=58 * 1024 * 1024
         ),
     )(queries, keys, values, out_cotangent, proj_weight)
-    return gq, gk, gv, gp.T
 
 
 def entering(part, axis, combine, identity, reverse):
@@ -508,7 +579,7 @@
 def per_device(n_seq, n_tp, *args):
     width, shard = args[0].shape[1], args[4].shape[1]
     groups = n_seq % (2 * PLANE) == 0 and n_tp == 2
-    if groups and shard % DH == 0 and width % (4 * DH * PARTS) == 0:
+    if groups and shard % DH == 0 and width % (2 * PLANE * DH) == 0:
         return fused(n_seq, *args)
     return gathered(*args)
 

time: 203 us -> 141 us (0.69)
  Pallas kernels: 196 us -> 133 us
    pallas_call x1, Pallas kernels: 196 us -> 133 us  [fused(): pl.pallas_call(functools.partial(kernel, depth, scale, proj_scale), out_s...]
where the time goes in v2:
time: 141 us
  Pallas kernels  133 us (94%)
  local copies, waits for them, and re-layouts  6.57 us (5%)
    pallas_call x1, Pallas kernels, fused(): pl.pallas_call(functools.partial(kernel, depth, scale, proj_scale), out_s...  133 us
    unnamed x10, local copies, waits for them, and re-layouts  6.57 us

profile of v2, /device:TPU:0, one launch (start us, length us, event | category | flops | bytes accessed | tf_op | source)
XLA Modules:
  0.0 140.6 jit_solution(765730346346885355)
XLA Ops:
  0.6 133.4 %shard_map.84 = (bf16[256,2048]{1,0:T(8,128)(2,1)}, bf16[256,2048]{1,0:T(8,128)(2,1)}, bf16[256,2048]{1,0:T(8,128)(2,1)}, f32[2048,128]{1,0:T(8,128)}) custom-call(bf16[256,2048]{1,0:T(8,128)(2,1)} %q.1, bf16[256,2048]{1,0:T(8,128)(2,1)} %k.1, bf16[256,2048]{1,0:T(8,128)(2,1)} %v.1, bf16[256,1024]{1,0:T(8,128)(2,1)} %c.1, bf16[2048,128]{1,0:T(8,128)(2,1)} %w.1), custom_call_target="tpu_custom_call" | custom-call | tf_op jit(solution)/shard_map/pallas_call | solution.py:459
  134.0 0.0 copy-start.2
  134.0 2.4 %copy.13 = bf16[256,2048]{1,0:T(8,128)(2,1)} copy(bf16[256,2048]{1,0:T(8,128)(2,1)} %get-tuple-element.8) | data formatting | bytes 2097152
  136.4 0.0 copy-done.2
  136.4 0.0 copy-start.1
  136.4 1.0 copy.14
  137.4 0.6 copy-done.1
  138.0 0.0 copy-start
  138.0 1.0 copy.15
  139.0 0.6 copy-done
  139.6 1.0 copy.16
Async XLA Ops:
  134.0 2.4 %copy-start.2 = (bf16[256,2048]{1,0:T(8,128)(2,1)S(1)}, bf16[256,2048]{1,0:T(8,128)(2,1)}, u32[]{:S(2)}) copy-start(bf16[256,2048]{1,0:T(8,128)(2,1)} %get-tuple-element.9) | copy-start | bytes 3145732
  136.4 1.6 %copy-start.1 = (bf16[256,2048]{1,0:T(8,128)(2,1)S(1)}, bf16[256,2048]{1,0:T(8,128)(2,1)}, u32[]{:S(2)}) copy-start(bf16[256,2048]{1,0:T(8,128)(2,1)} %get-tuple-element.10) | copy-start | bytes 3145732
  138.0 1.6 %copy-start = (f32[2048,128]{1,0:T(8,128)S(1)}, f32[2048,128]{1,0:T(8,128)}, u32[]{:S(2)}) copy-start(f32[2048,128]{1,0:T(8,128)} %get-tuple-element.11) | copy-start | bytes 3145732

commit v3 on v2

--- a/solution.py
+++ b/solution.py
@@ -50,7 +50,7 @@
     depth, scale, proj_scale,
     q, k, v, c, w,
     gq, gk, gv, gp,
-    csend, cbuf, ct, wall, attn_s, aall, gs1, gr1, gkeep, gs2, gr2, gfull, pacc, pown, pbf, precv,
+    csend, cbuf, ct, wall, attn_s, aall, gs1, gr1, gkeep, gs2, gr2, gfull, pacc, pbf, prel, psum, precv,
     gkpart, gvpart, st1, rv1, zs1, zr1, ps1, prior, st2, rv2, zs2, zr2, ps2, later, zacc,
     send_sem, recv_sem,
 ):
@@ -79,6 +79,11 @@
     def z_dev(zz):
         return (zz * PLANE + p, t)
 
+    pair = z // 2
+    mate = z + 1 - 2 * (z % 2)
+    far_in, far_out = 2 - pair, 3 - 3 * pair
+    inner, outer = z == 1 + pair, z == 3 * pair
+
     def up(j):
         return (z + j) % depth
 
@@ -92,27 +97,58 @@
     for dev in greet:
         pl.semaphore_signal(barrier, inc=1, device_id=dev, device_id_type=pl.DeviceIdType.MESH)
 
-    w_first = sems.take(3 * depth)
+    w_first = sems.take(15)
     w_cuts = (0, width // 4, width // 2, width)
 
-    def w_copy(part, j, slot):
+    def w_copy(part, i, owner, slot, to):
         rows = pl.ds(w_cuts[part], w_cuts[part + 1] - w_cuts[part])
-        return sems.copy(
-            w_first + part * depth + j,
-            w.at[rows, :],
-            wall.at[rows, lanes(slot * shard, shard)],
-            z_dev(up(j)),
-        )
+        there = wall.at[rows, lanes(slot * shard, shard)]
+        src = w.at[rows, :] if owner is None else wall.at[rows, lanes(owner * shard, shard)]
+        return sems.copy(w_first + 5 * part + i, src, there, z_dev(to))
+
+    def w_own(part, slot):
+        return w_copy(part, 0, None, slot, mate)
+
+    def w_far(part, i, slot):
+        return w_copy(part, 1 + i, None, slot, far_in)
+
+    def w_pass(part, i, owner, slot):
+        return w_copy(part, 3 + i, owner, slot, mate)
 
     def w_send(part):
-        for j in range(1, depth):
-            cp = w_copy(part, j, z)
-            cp.start()
-            started.append(cp)
+        for i, mine in enumerate((inner, outer)):
+            @pl.when(mine)
+            def _():
+                w_far(part, i, z).start()
+        cp = w_own(part, z)
+        cp.start()
+        started.append(cp)
+
+    def w_relay(part):
+        @pl.when(inner)
+        def _():
+            for i, owner in enumerate((far_in, far_out)):
+                w_far(part, i, owner).wait_recv()
+                w_pass(part, i, owner, owner).start()
 
     def w_wait(part):
-        for j in range(1, depth):
-            w_copy(part, j, down(j)).wait_recv()
+        w_own(part, mate).wait_recv()
+
+        @pl.when(outer)
+        def _():
+            for i, owner in enumerate((far_in, far_out)):
+                w_pass(part, i, owner, owner).wait_recv()
+
+    def w_sent(part):
+        for i, mine in enumerate((inner, outer)):
+            @pl.when(mine)
+            def _():
+                w_far(part, i, z).wait_send()
+
+        @pl.when(inner)
+        def _():
+            for i, owner in enumerate((far_in, far_out)):
+                w_pass(part, i, owner, owner).wait_send()
 
     per = half // shard
     for pp in range(PLANE):
@@ -253,6 +289,7 @@
         cp = c_pass(j, t)
         cp.start()
         started.append(cp)
+    w_relay(0)
 
     def out_head(h):
         cols = lanes(h * DH, DH)
@@ -294,7 +331,10 @@
         c_pass(j, 1 - t).wait_recv()
     for pp in range(PLANE):
         ct[:, pp * tok : (pp + 1) * tok] = cbuf[pp].T
+    w_relay(1)
     for part in range(PARTS):
+        if part == 2:
+            w_relay(2)
         via = 1 + part % 2
         a_copy(part, via, peer(via)).wait_recv()
         cp = a_pass(part, peer(via))
@@ -342,15 +382,26 @@
             total = gkeep[part, 0] + gr1[part, 0].astype(F32) + gr2[part].astype(F32)
             gfull[:, part * step : (part + 1) * step] = total.astype(BF16)
 
-    p_first = sems.take(PARTS * depth)
-
-    def p_copy(part, j, slot):
+    p_first = sems.take(4 * PARTS)
+    far = 2 - 2 * pair
+
+    def p_near(part):
         cols = pl.ds(part * step, step)
         return sems.copy(
-            p_first + part * depth + j,
-            pbf.at[up(j), :, cols],
-            precv.at[slot, :, cols],
-            z_dev(up(j)),
+            p_first + 4 * part, pbf.at[mate, :, cols], precv.at[0, :, cols], z_dev(mate)
+        )
+
+    def p_hand(part):
+        cols = pl.ds(part * step, step)
+        return sems.copy(
+            p_first + 4 * part + 1, pbf.at[pl.ds(far, 2), :, cols], prel.at[:, :, cols], z_dev(mate)
+        )
+
+    def p_far(part, i):
+        cols = pl.ds(part * step, step)
+        block, to = ((pair, far_in), (1 - pair, far_out))[i]
+        return sems.copy(
+            p_first + 4 * part + 2 + i, psum.at[block, :, cols], precv.at[1, :, cols], z_dev(to)
         )
 
     def p_part(part):
@@ -360,13 +411,45 @@
         cols = pl.ds(part * step, step)
         r = dot(ct[...], aall[:, :, cols].reshape(PLANE * tok, step), 1, 0)
         r = r.reshape(depth, shard, step)
-        pacc[...] = r
+        pacc[:, :, cols] = r
         pbf[:, :, cols] = r.astype(BF16)
-        pown[:, cols] = pacc[z]
-        for j in range(1, depth):
-            cp = p_copy(part, j, z)
-            cp.start()
-            started.append(cp)
+
+        @pl.when(outer)
+        def _():
+            p_hand(part).start()
+
+        cp = p_near(part)
+        cp.start()
+        started.append(cp)
+
+    def p_relay(part):
+        @pl.when(inner)
+        def _():
+            cols = pl.ds(part * step, step)
+            p_hand(part).wait_recv()
+            for i in range(2):
+                psum[i, :, cols] = (
+                    pacc[far + i, :, cols] + prel[i, :, cols].astype(F32)
+                ).astype(BF16)
+            for i in range(2):
+                p_far(part, i).start()
+
+    def p_done(part):
+        p_near(part).wait_recv()
+        for i, mine in enumerate((inner, outer)):
+            @pl.when(mine)
+            def _():
+                p_far(part, i).wait_recv()
+
+    def p_sent(part):
+        @pl.when(outer)
+        def _():
+            p_hand(part).wait_send()
+
+        @pl.when(inner)
+        def _():
+            for i in range(2):
+                p_far(part, i).wait_send()
 
     w_wait(0)
     w_wait(1)
@@ -376,6 +459,8 @@
     g_second_step(0)
     w_wait(2)
     g_first_step(1)
+    p_relay(0)
+    p_relay(1)
     p_part(2)
     p_part(3)
 
@@ -384,6 +469,8 @@
     scan_states(q, gfull, st2.at[0], 0)
     qg_cp[0] = scan_start(st2.at[0], rv2.at[0])
     g_second_step(1)
+    p_relay(2)
+    p_relay(3)
 
     def inner_head(h):
         cols = lanes(h * DH, DH)
@@ -404,14 +491,11 @@
     qg_later[0] = scan_spread(qg_z[0], rv2.at[0], zr2.at[0], ps2.at[0], later.at[0], True)
 
     for part in range(PARTS):
-        for j in range(1, depth):
-            p_copy(part, j, down(j)).wait_recv()
-
-    for part in range(PARTS):
         cols = pl.ds(part * step, step)
-        r = pown[:, cols]
-        for j in range(1, depth):
-            r = r + precv[down(j), :, cols].astype(F32)
+        p_done(part)
+        r = pacc[z, :, cols]
+        for i in range(2):
+            r = r + precv[i, :, cols].astype(F32)
         gp[cols, :] = (r * proj_scale).T
 
     def last_head(h):
@@ -430,9 +514,30 @@
 
     for cp in started:
         cp.wait_send()
+    for part in range(3):
+        w_sent(part)
+    for part in range(PARTS):
+        p_sent(part)
     for hi in range(2):
         scan_depth_sent(kv_z[hi], False)
         scan_depth_sent(qg_z[hi], True)
+
+
+def write_out(*arrays):
+    steps = 4
+
+    def body(*refs):
+        for src, dst in zip(refs[: len(arrays)], refs[len(arrays) :]):
+            dst[...] = src[...]
+
+    specs = [pl.BlockSpec((a.shape[0] // steps, a.shape[1]), lambda i: (i, 0)) for a in arrays]
+    return pl.pallas_call(
+        body,
+        grid=(steps,),
+        out_shape=tuple(jax.ShapeDtypeStruct(a.shape, a.dtype) for a in arrays),
+        in_specs=specs,
+        out_specs=tuple(specs),
+    )(*arrays)
 
 
 def fused(n_seq, queries, keys, values, out_cotangent, proj_weight):
@@ -456,7 +561,7 @@
     ]
     vmem = pl.BlockSpec(memory_space=pltpu.VMEM)
     grad = jax.ShapeDtypeStruct((tok, width), BF16)
-    return pl.pallas_call(
+    outs = pl.pallas_call(
         functools.partial(kernel, depth, scale, proj_scale),
         out_shape=(grad, grad, grad, jax.ShapeDtypeStruct((width, shard), F32)),
         in_specs=[vmem] * 5,
@@ -474,10 +579,11 @@
             bf(PARTS, tok, width // PARTS),
             bf(PARTS, tok, width // PARTS),
             bf(tok, width),
-            f32(depth, shard, width // PARTS),
-            f32(shard, width),
+            f32(depth, shard, width),
             bf(depth, shard, width),
-            bf(depth, shard, width),
+            bf(2, shard, width),
+            bf(2, shard, width),
+            bf(2, shard, width),
             f32(tok, width),
             f32(tok, width),
             *scan,
@@ -490,6 +596,7 @@
             collective_id=0, has_side_effects=True, vmem_limit_bytes=58 * 1024 * 1024
         ),
     )(queries, keys, values, out_cotangent, proj_weight)
+    return write_out(*outs)
 
 
 def entering(part, axis, combine, identity, reverse):
@@ -578,7 +685,7 @@
 
 def per_device(n_seq, n_tp, *args):
     width, shard = args[0].shape[1], args[4].shape[1]
-    groups = n_seq % (2 * PLANE) == 0 and n_tp == 2
+    groups = n_seq == PLANE * PLANE and n_tp == 2
     if groups and shard % DH == 0 and width % (2 * PLANE * DH) == 0:
         return fused(n_seq, *args)
     return gathered(*args)

time: 141 us -> 130 us (0.922)
  local copies, waits for them, and re-layouts: 6.57 us -> 0 us
  Pallas kernels: 133 us -> 129 us
    pallas_call x1, Pallas kernels: 133 us -> 125 us  [fused(): pl.pallas_call(functools.partial(kernel, depth, scale, proj_scale), out_s...]
    unnamed x10 -> x0, local copies, waits for them, and re-layouts: 6.57 us -> none
    pallas_call x0 -> x1, Pallas kernels: none -> 4.66 us  [write_out(): pl.pallas_call(body, grid=(steps,), out_shape=tuple((jax.ShapeDtypeStruct...]
where the time goes in v3:
time: 130 us
  Pallas kernels  129 us (99%)
    pallas_call x1, Pallas kernels, fused(): pl.pallas_call(functools.partial(kernel, depth, scale, proj_scale), out_s...  125 us
    pallas_call x1, Pallas kernels, write_out(): pl.pallas_call(body, grid=(steps,), out_shape=tuple((jax.ShapeDtypeStruct...  4.66 us

profile of v3, /device:TPU:0, one launch (start us, length us, event | category | flops | bytes accessed | tf_op | source)
XLA Modules:
  0.0 130.1 jit_solution(2797317757260740642)
XLA Ops:
  0.6 124.8 %shard_map.84 = (bf16[256,2048]{1,0:T(8,128)(2,1)}, bf16[256,2048]{1,0:T(8,128)(2,1)}, bf16[256,2048]{1,0:T(8,128)(2,1)}, f32[2048,128]{1,0:T(8,128)}) custom-call(bf16[256,2048]{1,0:T(8,128)(2,1)} %q.1, bf16[256,2048]{1,0:T(8,128)(2,1)} %k.1, bf16[256,2048]{1,0:T(8,128)(2,1)} %v.1, bf16[256,1024]{1,0:T(8,128)(2,1)} %c.1, bf16[2048,128]{1,0:T(8,128)(2,1)} %w.1), custom_call_target="tpu_custom_call" | custom-call | tf_op jit(solution)/shard_map/pallas_call | solution.py:564
  125.4 4.7 %shard_map.85 = (bf16[256,2048]{1,0:T(8,128)(2,1)}, bf16[256,2048]{1,0:T(8,128)(2,1)}, bf16[256,2048]{1,0:T(8,128)(2,1)}, f32[2048,128]{1,0:T(8,128)}) custom-call(bf16[256,2048]{1,0:T(8,128)(2,1)} %get-tuple-element.8.refs_0_, bf16[256,2048]{1,0:T(8,128)(2,1)} %get-tuple-element.9.refs_1_, bf16[256,2048]{1,0:T(8,128)(2,1)} %get-tuple-element.10.refs_2_, ...), custom_call_target="tpu_custom_call" | custom-call | tf_op jit(solution)/shard_map/pallas_call | solution.py:534

commit v4 on v3

--- a/solution.py
+++ b/solution.py
@@ -43,7 +43,7 @@
         )
 
 
-N_SEMS = 128
+N_SEMS = 176
 
 
 def kernel(
@@ -58,7 +58,7 @@
     p, z = s % PLANE, s // PLANE
     tok, width = q.shape
     heads = width // DH
-    hq = heads // (2 * PLANE)
+    hq = heads // (PARTS * PLANE)
     half = c.shape[1] // PLANE
     shard = w.shape[1]
     sems = Sems(send_sem, recv_sem)
@@ -184,7 +184,7 @@
             cols = lanes(h * DH, DH)
             st[h // hq % PLANE, h % hq] = dot(a[:, cols], b[:, cols], 0, 0).astype(BF16)
 
-        each_head(hi * heads // 2, (hi + 1) * heads // 2, one)
+        each_head(hi * heads // PARTS, (hi + 1) * heads // PARTS, one)
 
     def scan_start(st, rv):
         first = sems.take(PLANE)
@@ -258,8 +258,9 @@
     pl.semaphore_wait(barrier, len(greet))
     kv_cp[0] = scan_start(st1.at[0], rv1.at[0])
     w_send(0)
-    scan_states(k, v, st1.at[1], 1)
-    kv_cp[1] = scan_start(st1.at[1], rv1.at[1])
+    for part in range(1, PARTS):
+        scan_states(k, v, st1.at[part], part)
+        kv_cp[part] = scan_start(st1.at[part], rv1.at[part])
     cbuf[p, :, lanes(t * half, half)] = csend[p]
     for j in range(1, PLANE):
         cp = c_copy(j, p)
@@ -278,11 +279,21 @@
         cols = lanes(h * DH, DH)
         attn_s[h] = jnp.where(causal, dot(q[:, cols], k[:, cols], 1, 1), 0.0).astype(BF16)
 
-    each_head(0, heads // 2, attn_head)
-    for hi in range(2):
-        kv_z[hi] = scan_depth(kv_cp[hi], rv1.at[hi], zs1.at[hi], zr1.at[hi], False)
+    def kv_depth(part):
+        kv_z[part] = scan_depth(kv_cp[part], rv1.at[part], zs1.at[part], zr1.at[part], False)
+
+    def kv_spread(part):
+        kv_prior[part] = scan_spread(
+            kv_z[part], rv1.at[part], zr1.at[part], ps1.at[part], prior.at[part], False
+        )
+
+    for part in range(PARTS):
+        kv_depth(part)
     w_send(1)
     w_send(2)
+    each_head(0, heads // 2, attn_head)
+    kv_spread(0)
+    kv_spread(1)
     each_head(heads // 2, heads, attn_head)
     for j in range(1, PLANE):
         c_copy(j, peer(j)).wait_recv()
@@ -315,18 +326,16 @@
             plane_dev(3 - via),
         )
 
-    for hi in range(2):
-        kv_prior[hi] = scan_spread(
-            kv_z[hi], rv1.at[hi], zr1.at[hi], ps1.at[hi], prior.at[hi], False
-        )
+    for part in range(PARTS):
         for j in range(1, PLANE):
-            kv_prior[hi](j, peer(j)).wait_recv()
-        for part in (2 * hi, 2 * hi + 1):
-            each_head(part * heads // PARTS, (part + 1) * heads // PARTS, out_head)
-            for j in (1, 2):
-                cp = a_copy(part, j, p)
-                cp.start()
-                started.append(cp)
+            kv_prior[part](j, peer(j)).wait_recv()
+        each_head(part * heads // PARTS, (part + 1) * heads // PARTS, out_head)
+        for j in (1, 2):
+            cp = a_copy(part, j, p)
+            cp.start()
+            started.append(cp)
+        if part + 2 < PARTS:
+            kv_spread(part + 2)
     for j in range(PLANE):
         c_pass(j, 1 - t).wait_recv()
     for pp in range(PLANE):
@@ -375,12 +384,11 @@
             cp.start()
             started.append(cp)
 
-    def g_final(hi):
-        for part in (2 * hi, 2 * hi + 1):
-            g_copy1(part, 0).wait_recv()
-            g_copy2(part).wait_recv()
-            total = gkeep[part, 0] + gr1[part, 0].astype(F32) + gr2[part].astype(F32)
-            gfull[:, part * step : (part + 1) * step] = total.astype(BF16)
+    def g_final(part):
+        g_copy1(part, 0).wait_recv()
+        g_copy2(part).wait_recv()
+        total = gkeep[part, 0] + gr1[part, 0].astype(F32) + gr2[part].astype(F32)
+        gfull[:, part * step : (part + 1) * step] = total.astype(BF16)
 
     p_first = sems.take(4 * PARTS)
     far = 2 - 2 * pair
@@ -465,9 +473,21 @@
     p_part(3)
 
     qg_cp, qg_z, qg_later = {}, {}, {}
-    g_final(0)
-    scan_states(q, gfull, st2.at[0], 0)
-    qg_cp[0] = scan_start(st2.at[0], rv2.at[0])
+    def qg_start(part):
+        g_final(part)
+        scan_states(q, gfull, st2.at[part], part)
+        qg_cp[part] = scan_start(st2.at[part], rv2.at[part])
+
+    def qg_depth(part):
+        qg_z[part] = scan_depth(qg_cp[part], rv2.at[part], zs2.at[part], zr2.at[part], True)
+
+    def qg_spread(part):
+        qg_later[part] = scan_spread(
+            qg_z[part], rv2.at[part], zr2.at[part], ps2.at[part], later.at[part], True
+        )
+
+    qg_start(0)
+    qg_start(1)
     g_second_step(1)
     p_relay(2)
     p_relay(3)
@@ -482,13 +502,17 @@
         gvpart[:, cols] = dot(attn_s[h], gh, 0, 0)
 
     each_head(0, heads // 2, inner_head)
-    qg_z[0] = scan_depth(qg_cp[0], rv2.at[0], zs2.at[0], zr2.at[0], True)
-    g_final(1)
-    scan_states(q, gfull, st2.at[1], 1)
-    qg_cp[1] = scan_start(st2.at[1], rv2.at[1])
+    qg_depth(0)
+    qg_depth(1)
+    qg_start(2)
+    qg_start(3)
+    qg_spread(0)
+    qg_spread(1)
+    qg_depth(2)
+    qg_depth(3)
     each_head(heads // 2, heads, inner_head)
-    qg_z[1] = scan_depth(qg_cp[1], rv2.at[1], zs2.at[1], zr2.at[1], True)
-    qg_later[0] = scan_spread(qg_z[0], rv2.at[0], zr2.at[0], ps2.at[0], later.at[0], True)
+    qg_spread(2)
+    qg_spread(3)
 
     for part in range(PARTS):
         cols = pl.ds(part * step, step)
@@ -504,13 +528,10 @@
         gk[:, cols] = (scale * (gkpart[:, cols] + dot(v[:, cols], la, 1, 1))).astype(BF16)
         gv[:, cols] = (scale * (gvpart[:, cols] + dot(k[:, cols], la, 1, 0))).astype(BF16)
 
-    for j in range(1, PLANE):
-        qg_later[0](j, peer(j)).wait_recv()
-    each_head(0, heads // 2, last_head)
-    qg_later[1] = scan_spread(qg_z[1], rv2.at[1], zr2.at[1], ps2.at[1], later.at[1], True)
-    for j in range(1, PLANE):
-        qg_later[1](j, peer(j)).wait_recv()
-    each_head(heads // 2, heads, last_head)
+    for part in range(PARTS):
+        for j in range(1, PLANE):
+            qg_later[part](j, peer(j)).wait_recv()
+        each_head(part * heads // PARTS, (part + 1) * heads // PARTS, last_head)
 
     for cp in started:
         cp.wait_send()
@@ -518,32 +539,43 @@
         w_sent(part)
     for part in range(PARTS):
         p_sent(part)
-    for hi in range(2):
-        scan_depth_sent(kv_z[hi], False)
-        scan_depth_sent(qg_z[hi], True)
+    for part in range(PARTS):
+        scan_depth_sent(kv_z[part], False)
+        scan_depth_sent(qg_z[part], True)
 
 
 def write_out(*arrays):
-    steps = 4
+    cuts = 2
 
     def body(*refs):
-        for src, dst in zip(refs[: len(arrays)], refs[len(arrays) :]):
-            dst[...] = src[...]
-
-    specs = [pl.BlockSpec((a.shape[0] // steps, a.shape[1]), lambda i: (i, 0)) for a in arrays]
+        srcs, dsts, sem = refs[: len(arrays)], refs[len(arrays) : -1], refs[-1]
+        copies = []
+        for i, (src, dst) in enumerate(zip(srcs, dsts)):
+            size = src.shape[0] // cuts
+            for c in range(cuts):
+                rows = pl.ds(c * size, size)
+                copies.append(
+                    pltpu.make_async_copy(src.at[rows, :], dst.at[rows, :], sem.at[i * cuts + c])
+                )
+        for cp in copies:
+            cp.start()
+        for cp in copies:
+            cp.wait()
+
+    any_space = pl.BlockSpec(memory_space=pl.ANY)
     return pl.pallas_call(
         body,
-        grid=(steps,),
         out_shape=tuple(jax.ShapeDtypeStruct(a.shape, a.dtype) for a in arrays),
-        in_specs=specs,
-        out_specs=tuple(specs),
+        in_specs=[any_space] * len(arrays),
+        out_specs=(any_space,) * len(arrays),
+        scratch_shapes=[pltpu.SemaphoreType.DMA((cuts * len(arrays),))],
     )(*arrays)
 
 
 def fused(n_seq, queries, keys, values, out_cotangent, proj_weight):
     tok, width = queries.shape
     heads = width // DH
-    hq = heads // (2 * PLANE)
+    hq = heads // (PARTS * PLANE)
     depth = n_seq // PLANE
     half = out_cotangent.shape[1] // PLANE
     shard = proj_weight.shape[1]
@@ -552,12 +584,12 @@
     bf = lambda *dims: pltpu.VMEM(dims, BF16)
     f32 = lambda *dims: pltpu.VMEM(dims, F32)
     scan = [
-        bf(2, PLANE, hq, DH, DH),
-        bf(2, PLANE, hq, DH, DH),
-        bf(2, hq, DH, DH),
-        bf(2, depth, hq, DH, DH),
-        bf(2, PLANE, hq, DH, DH),
-        bf(2, PLANE, hq, DH, DH),
+        bf(PARTS, PLANE, hq, DH, DH),
+        bf(PARTS, PLANE, hq, DH, DH),
+        bf(PARTS, hq, DH, DH),
+        bf(PARTS, depth, hq, DH, DH),
+        bf(PARTS, PLANE, hq, DH, DH),
+        bf(PARTS, PLANE, hq, DH, DH),
     ]
     vmem = pl.BlockSpec(memory_space=pltpu.VMEM)
     grad = jax.ShapeDtypeStruct((tok, width), BF16)
@@ -686,7 +718,7 @@
 def per_device(n_seq, n_tp, *args):
     width, shard = args[0].shape[1], args[4].shape[1]
     groups = n_seq == PLANE * PLANE and n_tp == 2
-    if groups and shard % DH == 0 and width % (2 * PLANE * DH) == 0:
+    if groups and shard % DH == 0 and width % (PARTS * PLANE * DH) == 0:
         return fused(n_seq, *args)
     return gathered(*args)
 

time: 130 us -> 249 us (1.92)
  Pallas kernels: 129 us -> 248 us
    pallas_call x1, Pallas kernels: 4.66 us -> 128 us  [write_out(): pl.pallas_call(body, out_shape=tuple((jax.ShapeDtypeStruct(a.shape, a.dty...]
    pallas_call x1, Pallas kernels: 125 us -> 119 us  [fused(): pl.pallas_call(functools.partial(kernel, depth, scale, proj_scale), out_s...]
where the time goes in v4:
time: 249 us; the launch traced here: 248 us
  Pallas kernels  248 us (100%)
    pallas_call x1, Pallas kernels, write_out(): pl.pallas_call(body, out_shape=tuple((jax.ShapeDtypeStruct(a.shape, a.dty...  128 us
    pallas_call x1, Pallas kernels, fused(): pl.pallas_call(functools.partial(kernel, depth, scale, proj_scale), out_s...  119 us

profile of v4, /device:TPU:0, one launch (start us, length us, event | category | flops | bytes accessed | tf_op | source)
XLA Modules:
  0.0 248.5 jit_solution(7617332284094377661)
XLA Ops:
  0.6 119.5 %shard_map.84 = (bf16[256,2048]{1,0:T(8,128)(2,1)}, bf16[256,2048]{1,0:T(8,128)(2,1)}, bf16[256,2048]{1,0:T(8,128)(2,1)}, f32[2048,128]{1,0:T(8,128)}) custom-call(bf16[256,2048]{1,0:T(8,128)(2,1)} %q.1, bf16[256,2048]{1,0:T(8,128)(2,1)} %k.1, bf16[256,2048]{1,0:T(8,128)(2,1)} %v.1, bf16[256,1024]{1,0:T(8,128)(2,1)} %c.1, bf16[2048,128]{1,0:T(8,128)(2,1)} %w.1), custom_call_target="tpu_custom_call" | custom-call | tf_op jit(solution)/shard_map/pallas_call | solution.py:596
  120.1 128.2 %shard_map.85 = (bf16[256,2048]{1,0:T(8,128)(2,1)}, bf16[256,2048]{1,0:T(8,128)(2,1)}, bf16[256,2048]{1,0:T(8,128)(2,1)}, f32[2048,128]{1,0:T(8,128)}) custom-call(bf16[256,2048]{1,0:T(8,128)(2,1)} %get-tuple-element.8.refs_0_, bf16[256,2048]{1,0:T(8,128)(2,1)} %get-tuple-element.9.refs_1_, bf16[256,2048]{1,0:T(8,128)(2,1)} %get-tuple-element.10.refs_2_, ...), custom_call_target="tpu_custom_call" | custom-call | tf_op jit(solution)/shard_map/pallas_call | solution.py:566

commit v5 on v4

--- a/solution.py
+++ b/solution.py
@@ -546,29 +546,39 @@
 
 def write_out(*arrays):
     cuts = 2
+    count = len(arrays)
 
     def body(*refs):
-        srcs, dsts, sem = refs[: len(arrays)], refs[len(arrays) : -1], refs[-1]
-        copies = []
-        for i, (src, dst) in enumerate(zip(srcs, dsts)):
-            size = src.shape[0] // cuts
+        srcs, dsts, held = refs[:count], refs[count : 2 * count], refs[2 * count : 3 * count]
+        sem_in, sem_out = refs[3 * count :]
+        ins, outs = [], []
+        for i in range(count):
+            size = srcs[i].shape[0] // cuts
             for c in range(cuts):
-                rows = pl.ds(c * size, size)
-                copies.append(
-                    pltpu.make_async_copy(src.at[rows, :], dst.at[rows, :], sem.at[i * cuts + c])
-                )
-        for cp in copies:
+                rows, n = pl.ds(c * size, size), i * cuts + c
+                here = held[i].at[rows, :]
+                ins.append(pltpu.make_async_copy(srcs[i].at[rows, :], here, sem_in.at[n]))
+                outs.append(pltpu.make_async_copy(here, dsts[i].at[rows, :], sem_out.at[n]))
+        for cp in ins:
             cp.start()
-        for cp in copies:
+        for arrived, leaving in zip(ins, outs):
+            arrived.wait()
+            leaving.start()
+        for cp in outs:
             cp.wait()
 
     any_space = pl.BlockSpec(memory_space=pl.ANY)
     return pl.pallas_call(
         body,
         out_shape=tuple(jax.ShapeDtypeStruct(a.shape, a.dtype) for a in arrays),
-        in_specs=[any_space] * len(arrays),
-        out_specs=(any_space,) * len(arrays),
-        scratch_shapes=[pltpu.SemaphoreType.DMA((cuts * len(arrays),))],
+        in_specs=[any_space] * count,
+        out_specs=(any_space,) * count,
+        scratch_shapes=[
+            *(pltpu.VMEM(a.shape, a.dtype) for a in arrays),
+            pltpu.SemaphoreType.DMA((cuts * count,)),
+            pltpu.SemaphoreType.DMA((cuts * count,)),
+        ],
+        compiler_params=pltpu.CompilerParams(vmem_limit_bytes=16 * 1024 * 1024),
     )(*arrays)
 
 

time: 249 us -> 128 us (0.51)
  Pallas kernels: 248 us -> 122 us
  local copies, waits for them, and re-layouts: 0 us -> 4.89 us
    pallas_call x1, Pallas kernels: 128 us -> 2.42 us  [write_out(): pl.pallas_call(body, out_shape=tuple((jax.ShapeDtypeStruct(a.shape, a.dty...]
    unnamed x0 -> x8, local copies, waits for them, and re-layouts: none -> 4.89 us
where the time goes in v5:
time: 128 us
  Pallas kernels  122 us (95%)
  local copies, waits for them, and re-layouts  4.89 us (4%)
    pallas_call x1, Pallas kernels, fused(): pl.pallas_call(functools.partial(kernel, depth, scale, proj_scale), out_s...  119 us
    unnamed x8, local copies, waits for them, and re-layouts  4.89 us

profile of v5, /device:TPU:0, one launch (start us, length us, event | category | flops | bytes accessed | tf_op | source)
XLA Modules:
  0.0 127.6 jit_solution(10493974702057964393)
XLA Ops:
  0.6 119.5 %shard_map.84 = (bf16[256,2048]{1,0:T(8,128)(2,1)}, bf16[256,2048]{1,0:T(8,128)(2,1)}, bf16[256,2048]{1,0:T(8,128)(2,1)}, f32[2048,128]{1,0:T(8,128)}) custom-call(bf16[256,2048]{1,0:T(8,128)(2,1)} %q.1, bf16[256,2048]{1,0:T(8,128)(2,1)} %k.1, bf16[256,2048]{1,0:T(8,128)(2,1)} %v.1, bf16[256,1024]{1,0:T(8,128)(2,1)} %c.1, bf16[2048,128]{1,0:T(8,128)(2,1)} %w.1), custom_call_target="tpu_custom_call" | custom-call | tf_op jit(solution)/shard_map/pallas_call | solution.py:606
  120.1 0.0 copy-start
  120.1 1.2 copy-done
  121.4 0.0 copy-start.1
  121.4 1.2 copy-done.1
  122.6 0.0 copy-start.2
  122.6 1.2 copy-done.2
  123.8 0.0 copy-start.3
  123.8 1.2 copy-done.3
  125.0 2.4 %shard_map.85 = (bf16[256,2048]{1,0:T(8,128)(2,1)}, bf16[256,2048]{1,0:T(8,128)(2,1)}, bf16[256,2048]{1,0:T(8,128)(2,1)}, f32[2048,128]{1,0:T(8,128)}) custom-call(bf16[256,2048]{1,0:T(8,128)(2,1)S(1)} %copy-done, bf16[256,2048]{1,0:T(8,128)(2,1)S(1)} %copy-done.1, bf16[256,2048]{1,0:T(8,128)(2,1)S(1)} %copy-done.2, f32[2048,128]{1,0:T(8,128)S(1)} %copy-done.3), custom_call_target="tpu_custom_call" | custom-call | tf_op jit(solution)/shard_map/pallas_call | solution.py:571
Async XLA Ops:
  120.1 1.2 copy-start
  121.4 1.2 copy-start.1
  122.6 1.2 copy-start.2
  123.8 1.2 copy-start.3
